TPU v7x, 32 devices: a whole 2x2x4 slice. The times are simulated.
32 devices in a mesh: ab: 4 (over z), cd: 2 (over y), rep: 4 (over x, core).
Axes of the slice: x: 2, y: 2, z: 4, core: 2. Of those that a mesh axis runs over, the one named last changes fastest.
Arguments:
- amplitudes: bfloat16 [4, 512, 8192], P('rep', 'ab', 'cd'), may hold values from -6 to 6
- pair_irrep: int32 [4, 512], P('rep', 'ab'), may hold values from 0 to 7, as said below
- integrals: bfloat16 [2048, 8192], P('ab', 'cd'), may hold values from -0.0625 to 0.0625
- residual_in: bfloat16 [4, 512, 2048], P('rep', None, ('ab', 'cd')), may hold values from -6 to 6
Outputs:
- residual: bfloat16 [4, 512, 2048], P('rep', None, ('ab', 'cd'))
Inputs may be any that keep to these rules, and one draw needn't show every extreme that they name: For each j, among the 512 labels pair_irrep(l, j * 128 + t) over all layers l and 0 <= t < 128, exactly half are 0, and in one layer l (drawn) all 128 of them are 0.
All inputs are finite; a program needn't handle non-finite values.
Results may differ from a plain program's by a relative error of at most 0.001.
Values may be sent and summed in bfloat16 or wider, within the bound.
A program may use at most 64 MiB of HBM per device.

v0:
```python
import jax
import jax.numpy as jnp
from jax import lax
from jax.sharding import PartitionSpec as P


def local(amplitudes, pair_irrep, integrals, residual_in):
    gathered, labels = (
        lax.all_gather(amplitudes[0], "ab", axis=0, tiled=True),
        lax.all_gather(pair_irrep[0], "ab", axis=0, tiled=True),
    )
    summed = lax.psum_scatter(
        lax.dot_general(
            integrals, gathered, (((1,), (1,)), ((), ())), preferred_element_type=jnp.float32
        ),
        "cd",
        scatter_dimension=0,
        tiled=True,
    )
    ladder = summed.T
    is_active = labels == 0
    added = jnp.where(is_active[:, None], ladder, 0.0)
    return (residual_in[0].astype(jnp.float32) + added).astype(jnp.bfloat16)[None]


def solution(mesh):
    return jax.shard_map(
        local,
        mesh=mesh,
        in_specs=(
            P("rep", "ab", "cd"),
            P("rep", "ab"),
            P("ab", "cd"),
            P("rep", None, ("ab", "cd")),
        ),
        out_specs=P("rep", None, ("ab", "cd")),
        check_vma=False,
    )
```

profile of v0, /device:TPU:1, one launch (start us, length us, event | category | flops | bytes accessed | tf_op | source)
XLA Modules:
  0.0 126.4 jit_solution(9381681754807796166)
XLA Ops:
  6.5 0.0 all-gather.4.cloned.1.call-start
  6.5 0.7 all-gather.4.cloned.1.call-update
  7.3 0.0 copy-start
  7.3 0.0 copy-start.1
  7.3 0.0 reduce-scatter.2.cloned.1.call-start
  7.3 84.5 %all-gather.4.cloned.1.call-done = bf16[1,512,4096]{2,1,0:T(8,128)(2,1)} async-done(((bf16[1,128,4096]{2,1,0:T(8,128)(2,1)}), bf16[1,512,4096]{2,1,0:T(8,128)(2,1)}) %all-gather.4.cloned.1.call-update) | async-done | bytes 4194320 | tf_op jit(solution)/shard_map/all_gather | solution.py:9
  91.8 6.8 %fusion = f32[512,512]{1,0:T(8,128)} fusion(bf16[512,4096]{1,0:T(8,128)(2,1)} %param.6, bf16[1,512,4096]{2,1,0:T(8,128)(2,1)} %all-gather.4.cloned.1.call-done), kind=kOutput, calls=%fused_computation | convolution fusion | flops 2147483648 | bytes 9437184 | tf_op jit(solution)/shard_map/dot_general | solution.py:13
  98.6 0.0 reduce-scatter.2.cloned.1.call-update
  98.6 0.0 copy-done
  98.7 0.1 copy.5
  98.8 0.0 copy-done.1
  98.8 6.3 %all-gather = s32[1,512]{1,0:T(1,128)S(1)} all-gather(s32[1,128]{1,0:T(1,128)S(1)} %copy-done.1), channel_id=2, replica_groups=mesh['ab'=4,'cd'=2,'rep'=4] {'ab'}, dimensions={1}, use_global_device_ids=true | all-gather | bytes 2560 | tf_op jit(solution)/shard_map/all_gather | solution.py:10
  105.1 12.5 %reduce-scatter.2.cloned.1.call-done = f32[256,512]{1,0:T(8,128)} async-done(((f32[512,512]{1,0:T(8,128)}), f32[256,512]{1,0:T(8,128)}) %reduce-scatter.2.cloned.1.call-update) | async-done | bytes 524304 | tf_op jit(solution)/shard_map/reduce_scatter | solution.py:12
  117.6 1.1 fusion.3
  118.8 0.8 copy.6
  (1 shorter events, 0.0 us)
Async XLA Ops:
  6.5 85.3 %all-gather.4.cloned.1.call-start = ((), (), s32[]{:S(2)}) async-start(), calls=%async_computation.2 | async-start | bytes 5242880 | tf_op jit(solution)/shard_map/all_gather | solution.py:9
  7.3 91.4 %copy-start = (bf16[1,512,256]{2,1,0:T(8,128)(2,1)S(1)}, bf16[1,512,256]{2,1,0:T(8,128)(2,1)}, u32[]{:S(2)}) copy-start(bf16[1,512,256]{2,1,0:T(8,128)(2,1)} %param.7) | copy-start | bytes 786436
  7.3 91.5 %copy-start.1 = (s32[1,128]{1,0:T(1,128)S(1)}, s32[1,128]{1,0:T(1,128)}, u32[]{:S(2)}) copy-start(s32[1,128]{1,0:T(1,128)} %param.5) | copy-start | bytes 1540
  7.3 110.4 %reduce-scatter.2.cloned.1.call-start = ((), (), s32[]{:S(2)}) async-start(), calls=%async_computation.1 | async-start | bytes 1572864 | tf_op jit(solution)/shard_map/reduce_scatter | solution.py:12
Sparse Core Ops, SparseCore 0:
  8.9 82.8 all-gather.3
  98.8 18.8 reduce-scatter.1
where the time goes:
time: 127 us; the launch traced here: 126 us
  waiting for transfers between devices  97.7 us (77%)
  between operations  13.4 us (11%)
  matrix products  6.8 us (5%)
  blocking collectives  6.28 us (5%)
    all_gather x1, waiting for transfers between devices, local(): lax.all_gather(amplitudes[0], 'ab', axis=0, tiled=True)  84.5 us
    reduce_scatter x1, waiting for transfers between devices, local(): lax.psum_scatter(lax.dot_general(integrals, gathered, (((1,), (1,)), ((),...  12.5 us
    dot_general x1, matrix products, local(): lax.dot_general(integrals, gathered, (((1,), (1,)), ((), ())), preferred_...  6.8 us
    all_gather x1, blocking collectives, local(): lax.all_gather(pair_irrep[0], 'ab', axis=0, tiled=True)  6.28 us
  transfers between devices with their start and end apart: 2, of which 2 were waited for; matrix products, arithmetic and copies ran while one was open for 0% of the time, Pallas kernels for 0%

commit v1 on v0

v1 whole, which is shorter than its diff:
```python
import functools

import jax
import jax.numpy as jnp
from jax import lax
from jax.experimental import pallas as pl
from jax.experimental.pallas import tpu as pltpu
from jax.sharding import PartitionSpec as P

CORES = 2
CHUNKS = 4
F32 = jnp.float32
BF16 = jnp.bfloat16
NT = (((1,), (1,)), ((), ()))


def remote(src, dst, send, recv, peer):
    return pltpu.make_async_remote_copy(
        src_ref=src, dst_ref=dst, send_sem=send, recv_sem=recv,
        device_id=peer, device_id_type=pl.DeviceIdType.MESH,
    )


def kernel(
    nz, nc, nr,
    amp, lab, integ, res_in, out,
    v, res, raw, g, labels, acc, y_in, s1, x_in, full,
    v_sem, res_sem, own_sem, lab_own,
    lab_s, lab_r, ax_s, ax_r, ac_s, ac_r, fw_s, fw_r,
    up_s, dn_s, z_r, lup_s, ldn_s, lz_r,
    y_s, y_r, x_s, x_r, c_s, c_r,
):
    z, c, r = lax.axis_index("ab"), lax.axis_index("cd"), lax.axis_index("rep")
    nh = nr // CORES
    hi, lo = r // CORES, r % CORES
    mate = r + 1 - 2 * lo
    rows = amp.shape[1]
    half = amp.shape[2] // nh
    wide = half // CHUNKS
    kept = nr * rows // 2 // CORES
    cols = integ.shape[0] // nc

    def to_rep(i):
        return {"rep": i}

    def columns(h, q):
        return pl.ds(pl.multiple_of(h * half + q * wide, wide), wide)

    def layer_rows(i):
        return pl.ds(pl.multiple_of(i * rows, rows), rows)

    v_copy = [
        pltpu.make_async_copy(integ.at[:, columns(hi, q)], v.at[q], v_sem.at[q])
        for q in range(CHUNKS)
    ]
    own_copy = [
        pltpu.make_async_copy(
            amp.at[0, :, columns(hi, q)], raw.at[q, layer_rows(r)], own_sem.at[q]
        )
        for q in range(CHUNKS)
    ]
    res_copy = pltpu.make_async_copy(res_in.at[0], res, res_sem)
    lab_copy = pltpu.make_async_copy(lab, labels.at[z, r], lab_own)
    lab_copy.start()
    for q in range(CHUNKS):
        own_copy[q].start()

    barrier = pltpu.get_barrier_semaphore()
    for d in range(1, nr):
        pl.semaphore_signal(
            barrier, inc=1, device_id=to_rep(lax.rem(r + d, nr)),
            device_id_type=pl.DeviceIdType.MESH,
        )
    for d in range(1, nc):
        pl.semaphore_signal(
            barrier, inc=1, device_id={"cd": lax.rem(c + d, nc)},
            device_id_type=pl.DeviceIdType.MESH,
        )

    @pl.when(z > 0)
    def _():
        pl.semaphore_signal(
            barrier, inc=1, device_id={"ab": z - 1}, device_id_type=pl.DeviceIdType.MESH
        )

    @pl.when(z < nz - 1)
    def _():
        pl.semaphore_signal(
            barrier, inc=1, device_id={"ab": z + 1}, device_id_type=pl.DeviceIdType.MESH
        )

    ends = (z == 0).astype(jnp.int32) + (z == nz - 1).astype(jnp.int32)
    pl.semaphore_wait(barrier, nr - 1 + nc - 1 + 2 - ends)

    def lab_out(d):
        peer = lax.rem(r + d, nr)
        return remote(lab, labels.at[z, r], lab_s.at[d], lab_r.at[r], to_rep(peer))

    def lab_in(d):
        src = lax.rem(r + d, nr)
        ref = labels.at[z, src]
        return remote(ref, ref, lab_s.at[d], lab_r.at[src], to_rep(src))

    def amp_out(d, q):
        h = lax.rem(hi + d, nh)
        return remote(
            amp.at[0, :, columns(h, q)], raw.at[q, layer_rows(r)],
            ax_s.at[d, q], ax_r.at[hi, q], to_rep(h * CORES + lo),
        )

    def amp_in(d, q):
        h = lax.rem(hi + d, nh)
        ref = raw.at[q, layer_rows(h * CORES + lo)]
        return remote(ref, ref, ax_s.at[d, q], ax_r.at[h, q], to_rep(h * CORES + lo))

    def mate_out(q):
        return remote(
            amp.at[0, :, columns(hi, q)], raw.at[q, layer_rows(r)],
            ac_s.at[q], ac_r.at[q], to_rep(mate),
        )

    def mate_in(q):
        ref = raw.at[q, layer_rows(mate)]
        return remote(ref, ref, ac_s.at[q], ac_r.at[q], to_rep(mate))

    def fwd_out(d, q):
        h = lax.rem(hi + d, nh)
        ref = raw.at[q, layer_rows(h * CORES + lo)]
        return remote(ref, ref, fw_s.at[d, q], fw_r.at[h, q], to_rep(mate))

    def fwd_in(d, q):
        h = lax.rem(hi + d, nh)
        ref = raw.at[q, layer_rows(h * CORES + 1 - lo)]
        return remote(ref, ref, fw_s.at[d, q], fw_r.at[h, q], to_rep(mate))

    for d in range(1, nr):
        lab_out(d).start()
    for q in range(CHUNKS):
        for d in range(1, nh):
            amp_out(d, q).start()
        mate_out(q).start()
    for q in range(CHUNKS):
        v_copy[q].start()
    res_copy.start()

    def up(b, q):
        ref = g.at[b, q]
        return remote(ref, ref, up_s.at[b, q], z_r.at[b, q], {"ab": z + 1})

    def down(b, q):
        ref = g.at[b, q]
        return remote(ref, ref, dn_s.at[b, q], z_r.at[b, q], {"ab": z - 1})

    def lab_up(b):
        ref = labels.at[b]
        return remote(ref, ref, lup_s.at[b], lz_r.at[b], {"ab": z + 1})

    def lab_down(b):
        ref = labels.at[b]
        return remote(ref, ref, ldn_s.at[b], lz_r.at[b], {"ab": z - 1})

    lane = lax.broadcasted_iota(jnp.int32, (rows, rows), 1)
    sub = lax.broadcasted_iota(jnp.int32, (rows, rows), 0)
    before = (sub < lane).astype(F32).astype(BF16)
    diagonal = sub == lane

    def places(b):
        act = [(labels[b, i] == 0).astype(F32) for i in range(nr)]
        stacked = jnp.concatenate(act + [jnp.zeros((8 - nr % 8, rows), F32)], axis=0)
        within = jnp.dot(stacked.astype(BF16), before, preferred_element_type=F32)
        found, start = [], jnp.zeros((1, 1), F32)
        for i in range(nr):
            found.append(jnp.where(act[i] > 0, within[i:i + 1] + start, -1.0))
            start = start + jnp.sum(act[i], axis=1, keepdims=True)
        return found

    def y_out(b, d):
        to = lax.rem(c + d, nc)
        return remote(
            acc.at[b, pl.ds(pl.multiple_of(to * cols, cols), cols)], y_in.at[b, c],
            y_s.at[b, d], y_r.at[b, c], {"cd": to},
        )

    def y_arrive(b, d):
        src = lax.rem(c + d, nc)
        ref = y_in.at[b, src]
        return remote(ref, ref, y_s.at[b, d], y_r.at[b, src], {"cd": src})

    def x_out(b, d):
        h = lax.rem(hi + d, nh)
        return remote(
            s1.at[b], x_in.at[b, hi], x_s.at[b, d], x_r.at[b, hi], to_rep(h * CORES + lo)
        )

    def x_arrive(b, d):
        h = lax.rem(hi + d, nh)
        ref = x_in.at[b, h]
        return remote(ref, ref, x_s.at[b, d], x_r.at[b, h], to_rep(h * CORES + lo))

    def c_out(b):
        ref = full.at[b, lo]
        return remote(ref, ref, c_s.at[b], c_r.at[b], to_rep(mate))

    def c_arrive(b):
        ref = full.at[b, 1 - lo]
        return remote(ref, ref, c_s.at[b], c_r.at[b], to_rep(mate))

    def multiply(b, q):
        part = lax.dot_general(v[q], g[b, q], NT, preferred_element_type=F32)
        if q == 0:
            acc[b] = part
        else:
            acc[b] += part

    def send_y(b):
        for d in range(1, nc):
            y_out(b, d).start()

    def finish(b, phase):
        if phase == 1:
            mine = acc[b, pl.ds(pl.multiple_of(c * cols, cols), cols)]
            for d in range(1, nc):
                y_arrive(b, d).wait_recv()
                mine = mine + y_in[b, lax.rem(c + d, nc)]
            s1[b] = mine
            for d in range(1, nh):
                x_out(b, d).start()
        if phase == 2:
            total = s1[b]
            for d in range(1, nh):
                x_arrive(b, d).wait_recv()
                total = total + x_in[b, lax.rem(hi + d, nh)]
            full[b, lo] = total
            c_out(b).start()
        if phase == 3:
            found = places(b)
            row = jnp.zeros((1, rows), F32)
            for i in range(nr):
                row = row + jnp.where(r == i, found[i], 0.0)
            column = jnp.sum(jnp.where(diagonal, row, 0.0), axis=1, keepdims=True)
            place = lax.broadcasted_iota(jnp.int32, (rows, kept), 1).astype(F32)
            c_arrive(b).wait_recv()
            added = jnp.zeros((rows, cols), F32)
            for i in range(CORES):
                spread = (place + float(i * kept) == column).astype(F32).astype(BF16)
                left = full[b, i]
                for _ in range(3):
                    piece = left.astype(BF16)
                    left = left - piece.astype(F32)
                    added = added + lax.dot_general(
                        spread, piece, NT, preferred_element_type=F32
                    )
            at = pl.ds(pl.multiple_of(b * rows, rows), rows)
            out[0, at] = (res[at].astype(F32) + added).astype(BF16)

    lab_copy.wait()
    for d in range(1, nr):
        lab_in(d).wait_recv()

    @pl.when(z < nz - 1)
    def _():
        lab_up(z).start()

    @pl.when(z > 0)
    def _():
        lab_down(z).start()

    order = lax.broadcasted_iota(jnp.int32, (kept, rows), 0).astype(F32)
    order = order + (lo * kept).astype(F32)
    pick = jnp.concatenate(
        [(order == p).astype(F32).astype(BF16) for p in places(z)], axis=1
    )
    for q in range(CHUNKS):
        for d in range(1, nh):
            amp_in(d, q).wait_recv()
            fwd_out(d, q).start()
        own_copy[q].wait()
        mate_in(q).wait_recv()
        for d in range(1, nh):
            fwd_in(d, q).wait_recv()
        g[z, q] = jnp.dot(pick, raw[q], preferred_element_type=F32).astype(BF16)

        @pl.when(z < nz - 1)
        def _():
            up(z, q).start()

        @pl.when(z > 0)
        def _():
            down(z, q).start()

        v_copy[q].wait()
        multiply(z, q)
    send_y(z)
    res_copy.wait()

    def stage(s, carry):
        for q in range(CHUNKS):
            @pl.when(z - s >= 0)
            def _():
                b = z - s
                up_like = remote(
                    g.at[b, q], g.at[b, q], up_s.at[b, q], z_r.at[b, q], {"ab": z - 1}
                )
                up_like.wait_recv()

                @pl.when(z < nz - 1)
                def _():
                    up(b, q).start()

                multiply(b, q)

            @pl.when(z + s < nz)
            def _():
                b = z + s
                down_like = remote(
                    g.at[b, q], g.at[b, q], dn_s.at[b, q], z_r.at[b, q], {"ab": z + 1}
                )
                down_like.wait_recv()

                @pl.when(z > 0)
                def _():
                    down(b, q).start()

                multiply(b, q)

            if q == 0:
                @pl.when(z - s >= 0)
                def _():
                    b = z - s
                    remote(
                        labels.at[b], labels.at[b], lup_s.at[b], lz_r.at[b], {"ab": z - 1}
                    ).wait_recv()

                    @pl.when(z < nz - 1)
                    def _():
                        lab_up(b).start()

                @pl.when(z + s < nz)
                def _():
                    b = z + s
                    remote(
                        labels.at[b], labels.at[b], ldn_s.at[b], lz_r.at[b], {"ab": z + 1}
                    ).wait_recv()

                    @pl.when(z > 0)
                    def _():
                        lab_down(b).start()
            else:
                @pl.when(z - s + 1 >= 0)
                def _():
                    finish(z - s + 1, q)

                @pl.when((z + s - 1 < nz) & (s > 1))
                def _():
                    finish(z + s - 1, q)

        @pl.when(z - s >= 0)
        def _():
            send_y(z - s)

        @pl.when(z + s < nz)
        def _():
            send_y(z + s)

        return carry

    lax.fori_loop(1, nz, stage, 0)

    @pl.when((z == 0) | (z == nz - 1))
    def _():
        b = nz - 1 - z
        for phase in (1, 2, 3):
            finish(b, phase)

    for d in range(1, nr):
        lab_out(d).wait_send()
    for q in range(CHUNKS):
        for d in range(1, nh):
            amp_out(d, q).wait_send()
            fwd_out(d, q).wait_send()
        mate_out(q).wait_send()

    def drain(b, carry):
        @pl.when((b <= z) & (z < nz - 1))
        def _():
            lab_up(b).wait_send()
            for q in range(CHUNKS):
                up(b, q).wait_send()

        @pl.when((b >= z) & (z > 0))
        def _():
            lab_down(b).wait_send()
            for q in range(CHUNKS):
                down(b, q).wait_send()

        for d in range(1, nc):
            y_out(b, d).wait_send()
        for d in range(1, nh):
            x_out(b, d).wait_send()
        c_out(b).wait_send()
        return carry

    lax.fori_loop(0, nz, drain, 0)


def local(nz, nc, nr, amplitudes, pair_irrep, integrals, residual_in):
    _, rows, wide = amplitudes.shape
    nh = nr // CORES
    chunk = wide // nh // CHUNKS
    height = integrals.shape[0]
    cols = height // nc
    kept = nr * rows // 2 // CORES
    dma = pltpu.SemaphoreType.DMA
    vmem = pltpu.VMEM
    flops = 2 * nz * height * kept * chunk * CHUNKS
    return pl.pallas_call(
        functools.partial(kernel, nz, nc, nr),
        out_shape=jax.ShapeDtypeStruct(residual_in.shape, BF16),
        in_specs=[pl.BlockSpec(memory_space=pl.ANY)] * 4,
        out_specs=pl.BlockSpec(memory_space=pltpu.VMEM),
        scratch_shapes=[
            vmem((CHUNKS, height, chunk), BF16),
            vmem(residual_in.shape[1:], BF16),
            vmem((CHUNKS, nr * rows, chunk), BF16),
            vmem((nz, CHUNKS, kept, chunk), BF16),
            vmem((nz, nr, 1, rows), jnp.int32),
            vmem((nz, height, kept), F32),
            vmem((nz, nc, cols, kept), F32),
            vmem((nz, cols, kept), F32),
            vmem((nz, nh, cols, kept), F32),
            vmem((nz, CORES, cols, kept), F32),
            dma((CHUNKS,)), dma, dma((CHUNKS,)), dma,
            dma((nr,)), dma((nr,)),
            dma((nh, CHUNKS)), dma((nh, CHUNKS)),
            dma((CHUNKS,)), dma((CHUNKS,)),
            dma((nh, CHUNKS)), dma((nh, CHUNKS)),
            dma((nz, CHUNKS)), dma((nz, CHUNKS)), dma((nz, CHUNKS)),
            dma((nz,)), dma((nz,)), dma((nz,)),
            dma((nz, nc)), dma((nz, nc)),
            dma((nz, nh)), dma((nz, nh)),
            dma((nz,)), dma((nz,)),
        ],
        compiler_params=pltpu.CompilerParams(
            collective_id=0, has_side_effects=True, vmem_limit_bytes=48 * 2 ** 20
        ),
        cost_estimate=pl.CostEstimate(
            flops=flops, bytes_accessed=2 * height * wide, transcendentals=0
        ),
    )(amplitudes, pair_irrep, integrals, residual_in)


def solution(mesh):
    return jax.shard_map(
        functools.partial(local, mesh.shape["ab"], mesh.shape["cd"], mesh.shape["rep"]),
        mesh=mesh,
        in_specs=(
            P("rep", "ab", "cd"),
            P("rep", "ab"),
            P("ab", "cd"),
            P("rep", None, ("ab", "cd")),
        ),
        out_specs=P("rep", None, ("ab", "cd")),
        check_vma=False,
    )
```

time: 127 us -> 68.9 us (0.54)
  waiting for transfers between devices: 97.7 us -> 0 us
  Pallas kernels: 0 us -> 62.9 us
  between operations: 13.4 us -> 0.01 us
  matrix products: 6.8 us -> 0 us
  blocking collectives: 6.28 us -> 0 us
  local copies, waits for them, and re-layouts: 0.99 us -> 5.72 us
    all_gather x1 -> x0, waiting for transfers between devices: 84.5 us -> none  [local(): lax.all_gather(amplitudes[0], 'ab', axis=0, tiled=True)]
    pallas_call x0 -> x1, Pallas kernels: none -> 62.9 us  [local(): pl.pallas_call(functools.partial(kernel, nz, nc, nr), out_shape=jax.Shape...]
    reduce_scatter x1 -> x0, waiting for transfers between devices: 12.5 us -> none  [local(): lax.psum_scatter(lax.dot_general(integrals, gathered, (((1,), (1,)), ((),...]
    dot_general x1 -> x0, matrix products: 6.8 us -> none  [local(): lax.dot_general(integrals, gathered, (((1,), (1,)), ((), ())), preferred_...]
    all_gather x1 -> x0, blocking collectives: 6.28 us -> none  [local(): lax.all_gather(pair_irrep[0], 'ab', axis=0, tiled=True)]
    unnamed x5 -> x9, local copies, waits for them, and re-layouts: 0.15 us -> 5.72 us
  transfers between devices with their start and end apart: 2 -> 0, of which waited for: 2 -> 0; matrix products, arithmetic and copies ran while one was open for 0% -> 0% of each run, Pallas kernels for 0% -> 0%
where the time goes in v1:
time: 68.9 us; the launch traced here: 68.6 us
  Pallas kernels  62.9 us (91%)
  local copies, waits for them, and re-layouts  5.72 us (8%)
    pallas_call x1, Pallas kernels, local(): pl.pallas_call(functools.partial(kernel, nz, nc, nr), out_shape=jax.Shape...  62.9 us
    unnamed x9, local copies, waits for them, and re-layouts  5.72 us

profile of v1, /device:TPU:1, one launch (start us, length us, event | category | flops | bytes accessed | tf_op | source)
XLA Modules:
  0.0 68.6 jit_solution(12016425444171492285)
XLA Ops:
  0.0 0.0 copy-start
  0.0 2.2 %copy-done = bf16[512,4096]{1,0:T(8,128)(2,1)S(1)} copy-done((bf16[512,4096]{1,0:T(8,128)(2,1)S(1)}, bf16[512,4096]{1,0:T(8,128)(2,1)}, u32[]{:S(2)}) %copy-start) | copy-done | bytes 4194328
  2.2 0.0 copy-start.1
  2.2 1.2 %copy-done.1 = bf16[1,128,4096]{2,1,0:T(8,128)(2,1)S(1)} copy-done((bf16[1,128,4096]{2,1,0:T(8,128)(2,1)S(1)}, bf16[1,128,4096]{2,1,0:T(8,128)(2,1)}, u32[]{:S(2)}) %copy-start.1) | copy-done | bytes 1048600
  3.4 0.0 copy-start.2
  3.4 0.9 %copy-done.2 = bf16[1,512,256]{2,1,0:T(8,128)(2,1)S(1)} copy-done((bf16[1,512,256]{2,1,0:T(8,128)(2,1)S(1)}, bf16[1,512,256]{2,1,0:T(8,128)(2,1)}, u32[]{:S(2)}) %copy-start.2) | copy-done | bytes 262168
  4.4 0.0 copy-start.3
  4.4 0.7 copy-done.3
  5.0 62.9 %shard_map.46 = bf16[1,512,256]{2,1,0:T(8,128)(2,1)S(1)} custom-call(bf16[1,128,4096]{2,1,0:T(8,128)(2,1)S(1)} %copy-done.1, s32[1,128]{1,0:T(1,128)S(1)} %copy-done.3, bf16[512,4096]{1,0:T(8,128)(2,1)S(1)} %copy-done, bf16[1,512,256]{2,1,0:T(8,128)(2,1)S(1)} %copy-done.2), custom_call_target="tpu_custom_call" | custom-call | flops 1073741824 | bytes 4194304 | tf_op jit(solution)/shard_map/pallas_call | solution.py:416
  67.9 0.7 %copy.6 = bf16[1,512,256]{2,1,0:T(8,128)(2,1)} copy(bf16[1,512,256]{2,1,0:T(8,128)(2,1)S(1)} %shard_map.46) | data formatting | bytes 524288
Async XLA Ops:
  0.0 2.2 %copy-start = (bf16[512,4096]{1,0:T(8,128)(2,1)S(1)}, bf16[512,4096]{1,0:T(8,128)(2,1)}, u32[]{:S(2)}) copy-start(bf16[512,4096]{1,0:T(8,128)(2,1)} %integ.1) | copy-start | bytes 12582916
  2.2 1.2 %copy-start.1 = (bf16[1,128,4096]{2,1,0:T(8,128)(2,1)S(1)}, bf16[1,128,4096]{2,1,0:T(8,128)(2,1)}, u32[]{:S(2)}) copy-start(bf16[1,128,4096]{2,1,0:T(8,128)(2,1)} %amp.1) | copy-start | bytes 3145732
  3.4 0.9 %copy-start.2 = (bf16[1,512,256]{2,1,0:T(8,128)(2,1)S(1)}, bf16[1,512,256]{2,1,0:T(8,128)(2,1)}, u32[]{:S(2)}) copy-start(bf16[1,512,256]{2,1,0:T(8,128)(2,1)} %res_in.1) | copy-start | bytes 786436
  4.4 0.7 copy-start.3

commit v2 on v1

--- a/solution.py
+++ b/solution.py
@@ -9,6 +9,7 @@
 
 CORES = 2
 CHUNKS = 4
+SPLIT = 2
 F32 = jnp.float32
 BF16 = jnp.bfloat16
 NT = (((1,), (1,)), ((), ()))
@@ -39,6 +40,7 @@
     wide = half // CHUNKS
     kept = nr * rows // 2 // CORES
     cols = integ.shape[0] // nc
+    part = cols // SPLIT
 
     def to_rep(i):
         return {"rep": i}
@@ -174,36 +176,38 @@
             start = start + jnp.sum(act[i], axis=1, keepdims=True)
         return found
 
-    def y_out(b, d):
+    def y_out(b, d, k):
         to = lax.rem(c + d, nc)
+        at = pl.ds(pl.multiple_of(to * cols + k * part, part), part)
         return remote(
-            acc.at[b, pl.ds(pl.multiple_of(to * cols, cols), cols)], y_in.at[b, c],
-            y_s.at[b, d], y_r.at[b, c], {"cd": to},
-        )
-
-    def y_arrive(b, d):
+            acc.at[b, at], y_in.at[b, c, pl.ds(k * part, part)],
+            y_s.at[b, d, k], y_r.at[b, c, k], {"cd": to},
+        )
+
+    def y_arrive(b, d, k):
         src = lax.rem(c + d, nc)
-        ref = y_in.at[b, src]
-        return remote(ref, ref, y_s.at[b, d], y_r.at[b, src], {"cd": src})
-
-    def x_out(b, d):
+        ref = y_in.at[b, src, pl.ds(k * part, part)]
+        return remote(ref, ref, y_s.at[b, d, k], y_r.at[b, src, k], {"cd": src})
+
+    def x_out(b, d, k):
         h = lax.rem(hi + d, nh)
         return remote(
-            s1.at[b], x_in.at[b, hi], x_s.at[b, d], x_r.at[b, hi], to_rep(h * CORES + lo)
-        )
-
-    def x_arrive(b, d):
-        h = lax.rem(hi + d, nh)
-        ref = x_in.at[b, h]
-        return remote(ref, ref, x_s.at[b, d], x_r.at[b, h], to_rep(h * CORES + lo))
-
-    def c_out(b):
-        ref = full.at[b, lo]
-        return remote(ref, ref, c_s.at[b], c_r.at[b], to_rep(mate))
-
-    def c_arrive(b):
-        ref = full.at[b, 1 - lo]
-        return remote(ref, ref, c_s.at[b], c_r.at[b], to_rep(mate))
+            s1.at[b, pl.ds(k * part, part)], x_in.at[b, hi, pl.ds(k * part, part)],
+            x_s.at[b, d, k], x_r.at[b, hi, k], to_rep(h * CORES + lo),
+        )
+
+    def x_arrive(b, d, k):
+        h = lax.rem(hi + d, nh)
+        ref = x_in.at[b, h, pl.ds(k * part, part)]
+        return remote(ref, ref, x_s.at[b, d, k], x_r.at[b, h, k], to_rep(h * CORES + lo))
+
+    def c_out(b, k):
+        ref = full.at[b, lo, pl.ds(k * part, part)]
+        return remote(ref, ref, c_s.at[b, k], c_r.at[b, k], to_rep(mate))
+
+    def c_arrive(b, k):
+        ref = full.at[b, 1 - lo, pl.ds(k * part, part)]
+        return remote(ref, ref, c_s.at[b, k], c_r.at[b, k], to_rep(mate))
 
     def multiply(b, q):
         part = lax.dot_general(v[q], g[b, q], NT, preferred_element_type=F32)
@@ -213,25 +217,29 @@
             acc[b] += part
 
     def send_y(b):
-        for d in range(1, nc):
-            y_out(b, d).start()
+        for k in range(SPLIT):
+            for d in range(1, nc):
+                y_out(b, d, k).start()
 
     def finish(b, phase):
         if phase == 1:
-            mine = acc[b, pl.ds(pl.multiple_of(c * cols, cols), cols)]
-            for d in range(1, nc):
-                y_arrive(b, d).wait_recv()
-                mine = mine + y_in[b, lax.rem(c + d, nc)]
-            s1[b] = mine
-            for d in range(1, nh):
-                x_out(b, d).start()
+            for k in range(SPLIT):
+                at = pl.ds(pl.multiple_of(c * cols + k * part, part), part)
+                mine = acc[b, at]
+                for d in range(1, nc):
+                    y_arrive(b, d, k).wait_recv()
+                    mine = mine + y_in[b, lax.rem(c + d, nc), pl.ds(k * part, part)]
+                s1[b, pl.ds(k * part, part)] = mine
+                for d in range(1, nh):
+                    x_out(b, d, k).start()
         if phase == 2:
-            total = s1[b]
-            for d in range(1, nh):
-                x_arrive(b, d).wait_recv()
-                total = total + x_in[b, lax.rem(hi + d, nh)]
-            full[b, lo] = total
-            c_out(b).start()
+            for k in range(SPLIT):
+                total = s1[b, pl.ds(k * part, part)]
+                for d in range(1, nh):
+                    x_arrive(b, d, k).wait_recv()
+                    total = total + x_in[b, lax.rem(hi + d, nh), pl.ds(k * part, part)]
+                full[b, lo, pl.ds(k * part, part)] = total
+                c_out(b, k).start()
         if phase == 3:
             found = places(b)
             row = jnp.zeros((1, rows), F32)
@@ -239,7 +247,8 @@
                 row = row + jnp.where(r == i, found[i], 0.0)
             column = jnp.sum(jnp.where(diagonal, row, 0.0), axis=1, keepdims=True)
             place = lax.broadcasted_iota(jnp.int32, (rows, kept), 1).astype(F32)
-            c_arrive(b).wait_recv()
+            for k in range(SPLIT):
+                c_arrive(b, k).wait_recv()
             added = jnp.zeros((rows, cols), F32)
             for i in range(CORES):
                 spread = (place + float(i * kept) == column).astype(F32).astype(BF16)
@@ -393,11 +402,12 @@
             for q in range(CHUNKS):
                 down(b, q).wait_send()
 
-        for d in range(1, nc):
-            y_out(b, d).wait_send()
-        for d in range(1, nh):
-            x_out(b, d).wait_send()
-        c_out(b).wait_send()
+        for k in range(SPLIT):
+            for d in range(1, nc):
+                y_out(b, d, k).wait_send()
+            for d in range(1, nh):
+                x_out(b, d, k).wait_send()
+            c_out(b, k).wait_send()
         return carry
 
     lax.fori_loop(0, nz, drain, 0)
@@ -416,7 +426,7 @@
     return pl.pallas_call(
         functools.partial(kernel, nz, nc, nr),
         out_shape=jax.ShapeDtypeStruct(residual_in.shape, BF16),
-        in_specs=[pl.BlockSpec(memory_space=pl.ANY)] * 4,
+        in_specs=[pl.BlockSpec(memory_space=pltpu.HBM)] * 4,
         out_specs=pl.BlockSpec(memory_space=pltpu.VMEM),
         scratch_shapes=[
             vmem((CHUNKS, height, chunk), BF16),
@@ -436,12 +446,12 @@
             dma((nh, CHUNKS)), dma((nh, CHUNKS)),
             dma((nz, CHUNKS)), dma((nz, CHUNKS)), dma((nz, CHUNKS)),
             dma((nz,)), dma((nz,)), dma((nz,)),
-            dma((nz, nc)), dma((nz, nc)),
-            dma((nz, nh)), dma((nz, nh)),
-            dma((nz,)), dma((nz,)),
+            dma((nz, nc, SPLIT)), dma((nz, nc, SPLIT)),
+            dma((nz, nh, SPLIT)), dma((nz, nh, SPLIT)),
+            dma((nz, SPLIT)), dma((nz, SPLIT)),
         ],
         compiler_params=pltpu.CompilerParams(
-            collective_id=0, has_side_effects=True, vmem_limit_bytes=48 * 2 ** 20
+            collective_id=0, has_side_effects=True, vmem_limit_bytes=62 * 2 ** 20
         ),
         cost_estimate=pl.CostEstimate(
             flops=flops, bytes_accessed=2 * height * wide, transcendentals=0

time: 68.9 us -> 61.4 us (0.89)
  local copies, waits for them, and re-layouts: 5.72 us -> 1.67 us
  Pallas kernels: 62.9 us -> 59.6 us
    unnamed x9 -> x1, local copies, waits for them, and re-layouts: 5.72 us -> 1.67 us
    pallas_call x1, Pallas kernels: 62.9 us -> 59.6 us  [local(): pl.pallas_call(functools.partial(kernel, nz, nc, nr), out_shape=jax.Shape...]
where the time goes in v2:
time: 61.4 us; the launch traced here: 61.3 us
  Pallas kernels  59.6 us (97%)
  local copies, waits for them, and re-layouts  1.67 us (3%)
    pallas_call x1, Pallas kernels, local(): pl.pallas_call(functools.partial(kernel, nz, nc, nr), out_shape=jax.Shape...  59.6 us
    unnamed x1, local copies, waits for them, and re-layouts  1.67 us

profile of v2, /device:TPU:1, one launch (start us, length us, event | category | flops | bytes accessed | tf_op | source)
XLA Modules:
  0.0 61.3 jit_solution(14039992712329739643)
XLA Ops:
  0.0 59.6 %shard_map.46 = bf16[1,512,256]{2,1,0:T(8,128)(2,1)} custom-call(bf16[1,128,4096]{2,1,0:T(8,128)(2,1)} %amp.1, s32[1,128]{1,0:T(1,128)} %lab.1, bf16[512,4096]{1,0:T(8,128)(2,1)} %integ.1, bf16[1,512,256]{2,1,0:T(8,128)(2,1)} %res_in.1), custom_call_target="tpu_custom_call" | custom-call | flops 1073741824 | bytes 4194304 | tf_op jit(solution)/shard_map/pallas_call | solution.py:426
  59.6 1.7 %copy.6 = bf16[1,512,256]{2,1,0:T(8,128)(2,1)} copy(bf16[1,512,256]{2,1,0:T(8,128)(2,1)} %shard_map.46) | data formatting | bytes 524288

commit v3 on v2

--- a/solution.py
+++ b/solution.py
@@ -375,11 +375,15 @@
 
     lax.fori_loop(1, nz, stage, 0)
 
-    @pl.when((z == 0) | (z == nz - 1))
-    def _():
-        b = nz - 1 - z
-        for phase in (1, 2, 3):
-            finish(b, phase)
+    at_end = (z == 0) | (z == nz - 1)
+
+    def sums_left(b):
+        for k in range(SPLIT):
+            for d in range(1, nc):
+                y_out(b, d, k).wait_send()
+            for d in range(1, nh):
+                x_out(b, d, k).wait_send()
+            c_out(b, k).wait_send()
 
     for d in range(1, nr):
         lab_out(d).wait_send()
@@ -402,15 +406,20 @@
             for q in range(CHUNKS):
                 down(b, q).wait_send()
 
-        for k in range(SPLIT):
-            for d in range(1, nc):
-                y_out(b, d, k).wait_send()
-            for d in range(1, nh):
-                x_out(b, d, k).wait_send()
-            c_out(b, k).wait_send()
+        @pl.when(~at_end | (b != nz - 1 - z))
+        def _():
+            sums_left(b)
+
         return carry
 
     lax.fori_loop(0, nz, drain, 0)
+
+    @pl.when(at_end)
+    def _():
+        b = nz - 1 - z
+        for phase in (1, 2, 3):
+            finish(b, phase)
+        sums_left(b)
 
 
 def local(nz, nc, nr, amplitudes, pair_irrep, integrals, residual_in):

time: 61.4 us -> 61.3 us (level)
  no operation moved by 1% of the time
where the time goes in v3:
time: 61.3 us; the launch traced here: 61.2 us
  Pallas kernels  59.5 us (97%)
  local copies, waits for them, and re-layouts  1.67 us (3%)
    pallas_call x1, Pallas kernels, local(): pl.pallas_call(functools.partial(kernel, nz, nc, nr), out_shape=jax.Shape...  59.5 us
    unnamed x1, local copies, waits for them, and re-layouts  1.67 us

profile of v3, /device:TPU:1, one launch (start us, length us, event | category | flops | bytes accessed | tf_op | source)
XLA Modules:
  0.0 61.2 jit_solution(16382736788509621092)
XLA Ops:
  0.0 59.5 %shard_map.46 = bf16[1,512,256]{2,1,0:T(8,128)(2,1)} custom-call(bf16[1,128,4096]{2,1,0:T(8,128)(2,1)} %amp.1, s32[1,128]{1,0:T(1,128)} %lab.1, bf16[512,4096]{1,0:T(8,128)(2,1)} %integ.1, bf16[1,512,256]{2,1,0:T(8,128)(2,1)} %res_in.1), custom_call_target="tpu_custom_call" | custom-call | flops 1073741824 | bytes 4194304 | tf_op jit(solution)/shard_map/pallas_call | solution.py:435
  59.5 1.7 %copy.6 = bf16[1,512,256]{2,1,0:T(8,128)(2,1)} copy(bf16[1,512,256]{2,1,0:T(8,128)(2,1)} %shard_map.46) | data formatting | bytes 524288
